TPU v7x, 512 devices: a whole 4x8x8 slice. The times are simulated.
512 devices in a mesh: expert: 64 (over x, z, core), replica: 8 (over y).
Axes of the slice: x: 4, y: 8, z: 8, core: 2. Of those that a mesh axis runs over, the one named last changes fastest.
Arguments:
- tokens: bfloat16 [768, 3584], P('expert', 'replica'), may hold values from -6 to 6
- expert_ids: int32 [768, 8], P('expert'), may hold values from 0 to 31, all different within a row; in each aligned block of 12 rows (0 to 11, 12 to 23, ...) at most 4 rows name the same one
- gate_values: float32 [768, 8], P('expert'), may hold values from 0.1 to 0.6
- gate_weight: bfloat16 [64, 512, 3584], P('expert', 'replica'), may hold values from -0.09375 to 0.09375
- up_weight: bfloat16 [64, 512, 3584], P('expert', 'replica'), may hold values from -0.09375 to 0.09375
- down_weight: bfloat16 [64, 512, 3584], P('expert', None, 'replica'), may hold values from -0.1875 to 0.1875
- out_grad: bfloat16 [768, 3584], P('expert', 'replica'), may hold values from -1.5 to 1.5
Outputs:
- moe_out: bfloat16 [768, 3584], P('expert', 'replica')
- token_grad: bfloat16 [768, 3584], P('expert', 'replica')
- gate_grad: bfloat16 [64, 512, 3584], P('expert', 'replica')
- up_grad: bfloat16 [64, 512, 3584], P('expert', 'replica')
- down_grad: bfloat16 [64, 512, 3584], P('expert', None, 'replica')
Inputs may be any that keep to these rules, and one draw needn't show every extreme that they name: `expert_ids`: each row names 8 different experts. Among the 12 rows of one index of expert, no expert is named by more than 4 rows, a bound that some block reaches.
All inputs are finite; a program needn't handle non-finite values.
Results may differ from a plain program's by a relative error of at most 0.0075.
Values may be sent and summed in bfloat16 or wider, within the bound.
A program may use at most 64 MiB of HBM per device.

v0:
```python
import jax
import jax.numpy as jnp
from jax import lax
from jax.sharding import PartitionSpec as P


def partner_2(block, axis, distance):
    count = lax.axis_size(axis)
    route = []
    for low in range(count):
        high = low | 1 << distance
        if high != low and high < count:
            route += [(low, high), (high, low)]
    return lax.ppermute(block, axis, route)


def pair_join(parity_bit, own_part, peer_part, stack_axis):
    first_part = jnp.where(parity_bit == 0, own_part, peer_part)
    second_part = jnp.where(parity_bit == 0, peer_part, own_part)
    return jnp.stack([first_part, second_part], axis=stack_axis)


def pick_half(parity_bit, stacked, stack_axis):
    lower = jnp.take(stacked, 0, axis=stack_axis)
    higher = jnp.take(stacked, 1, axis=stack_axis)
    return (jnp.where(parity_bit == 0, lower, higher), jnp.where(parity_bit == 0, higher, lower))


def per_device(tokens, expert_ids, gate_values, gate_weight, up_weight, down_weight, out_grad):
    experts_axis = lax.axis_size("expert")
    tok_rows, slice_width = tokens.shape
    top_count = expert_ids.shape[1]
    expert_count = experts_axis // 2
    most_rows = min(tok_rows, 4 * tok_rows * top_count // (3 * expert_count))
    capacity = (most_rows + 1) // 2
    pair_count = tok_rows * top_count
    slot_count = experts_axis * capacity
    flat_ids = expert_ids.reshape(pair_count)
    onehot = (flat_ids[:, None] == jnp.arange(expert_count, dtype=jnp.int32)[None, :]).astype(
        jnp.int32
    )
    rank_in = jnp.sum((jnp.cumsum(onehot, axis=0) - onehot) * onehot, axis=1)
    upper_copy = (rank_in >= capacity).astype(jnp.int32)
    target = (2 * flat_ids + upper_copy) * capacity + rank_in - upper_copy * capacity
    slot_match = target[None, :] == jnp.arange(slot_count, dtype=jnp.int32)[:, None]
    filled = jnp.any(slot_match, axis=1)
    source_pair = jnp.sum(
        jnp.where(slot_match, jnp.arange(pair_count, dtype=jnp.int32)[None, :], 0), axis=1
    )
    source_token = source_pair // top_count
    flat_gates = gate_values.reshape(pair_count)
    send_rows = jnp.where(filled[:, None], tokens[source_token], jnp.zeros((), tokens.dtype))
    scaled = flat_gates[source_pair][:, None] * out_grad[source_token].astype(jnp.float32)
    send_grads = jnp.where(filled[:, None], scaled, 0.0).astype(jnp.bfloat16)
    got_rows, got_grads = (
        lax.all_to_all(
            send_rows.reshape(experts_axis, capacity, slice_width),
            "expert",
            split_axis=0,
            concat_axis=0,
            tiled=True,
        ),
        lax.all_to_all(
            send_grads.reshape(experts_axis, capacity, slice_width),
            "expert",
            split_axis=0,
            concat_axis=0,
            tiled=True,
        ),
    )
    rows_part = got_rows.reshape(slot_count, slice_width)
    grads_part = got_grads.reshape(slot_count, slice_width)
    parity_bit = lax.axis_index("expert") % 2
    own_pieces = (gate_weight[0], up_weight[0], down_weight[0])
    partner = partner_2((own_pieces[0], own_pieces[1], own_pieces[2]), "expert", 0)
    w_gate = pair_join(parity_bit, own_pieces[0], partner[0], 0)
    w_up = pair_join(parity_bit, own_pieces[1], partner[1], 0)
    w_down = pair_join(parity_bit, own_pieces[2], partner[2], 0)
    _, quarter, model_width = w_gate.shape
    full_rows = lax.all_gather(rows_part, "replica", axis=1, tiled=True)
    contract = (((1,), (1,)), ((), ()))
    pre_gate = lax.dot_general(
        full_rows,
        w_gate.reshape(2 * quarter, model_width),
        contract,
        preferred_element_type=jnp.float32,
    ).reshape(slot_count, 2, quarter)
    pre_up = lax.dot_general(
        full_rows,
        w_up.reshape(2 * quarter, model_width),
        contract,
        preferred_element_type=jnp.float32,
    ).reshape(slot_count, 2, quarter)
    sigma = jax.nn.sigmoid(pre_gate)
    activated = pre_gate * sigma
    slope_term = sigma * (1.0 + pre_gate * (1.0 - sigma))
    hidden = (activated * pre_up).astype(jnp.bfloat16)
    all_hidden = lax.all_gather(hidden, "replica", axis=2, tiled=True).reshape(slot_count, -1)
    down_full = w_down.reshape(-1, slice_width)
    expert_out = jnp.dot(all_hidden, down_full, preferred_element_type=jnp.float32).astype(
        jnp.bfloat16
    )
    returned = lax.all_to_all(
        expert_out.reshape(experts_axis, capacity, slice_width),
        "expert",
        split_axis=0,
        concat_axis=0,
        tiled=True,
    ).reshape(slot_count, slice_width)
    picked = returned[target].astype(jnp.float32).reshape(tok_rows, top_count, slice_width)
    moe_out = jnp.sum(picked * gate_values[:, :, None], axis=1).astype(jnp.bfloat16)
    down_local = lax.dot_general(
        all_hidden, grads_part, (((0,), (0,)), ((), ())), preferred_element_type=jnp.float32
    )
    full_grads = lax.all_gather(grads_part, "replica", axis=1, tiled=True)
    down_rows = lax.all_to_all(w_down, "replica", split_axis=1, concat_axis=2, tiled=True)
    hidden_grad = jnp.einsum(
        "sd,hqd->shq", full_grads, down_rows, preferred_element_type=jnp.float32
    )
    gate_act = (hidden_grad * pre_up * slope_term).astype(jnp.bfloat16)
    up_act = (hidden_grad * activated).astype(jnp.bfloat16)
    gate_local = jnp.einsum("sd,shq->hqd", full_rows, gate_act, preferred_element_type=jnp.float32)
    up_local = jnp.einsum("sd,shq->hqd", full_rows, up_act, preferred_element_type=jnp.float32)
    all_gate_act, all_up_act = (
        lax.all_gather(gate_act, "replica", axis=2, tiled=True),
        lax.all_gather(up_act, "replica", axis=2, tiled=True),
    )
    rows_gate, rows_up = (
        lax.all_to_all(w_gate, "replica", split_axis=2, concat_axis=1, tiled=True),
        lax.all_to_all(w_up, "replica", split_axis=2, concat_axis=1, tiled=True),
    )
    input_rows = jnp.einsum(
        "shf,hfd->sd", all_gate_act, rows_gate, preferred_element_type=jnp.float32
    )
    input_rows = input_rows + jnp.einsum(
        "shf,hfd->sd", all_up_act, rows_up, preferred_element_type=jnp.float32
    )
    grads_back = lax.all_to_all(
        input_rows.astype(jnp.bfloat16).reshape(experts_axis, capacity, slice_width),
        "expert",
        split_axis=0,
        concat_axis=0,
        tiled=True,
    ).reshape(slot_count, slice_width)
    token_grad = jnp.sum(
        grads_back[target].astype(jnp.float32).reshape(tok_rows, top_count, slice_width), axis=1
    ).astype(jnp.bfloat16)
    keep_gate, give_gate = pick_half(parity_bit, gate_local, 0)
    keep_up, give_up = pick_half(parity_bit, up_local, 0)
    keep_down, give_down = pick_half(parity_bit, down_local.reshape(2, -1, slice_width), 0)
    received = (
        partner_2(give_gate.astype(jnp.bfloat16), "expert", 0).astype(give_gate.dtype),
        partner_2(give_up.astype(jnp.bfloat16), "expert", 0).astype(give_up.dtype),
        partner_2(give_down.astype(jnp.bfloat16), "expert", 0).astype(give_down.dtype),
    )
    gate_grad = (keep_gate + received[0]).astype(jnp.bfloat16)[None]
    up_grad = (keep_up + received[1]).astype(jnp.bfloat16)[None]
    down_grad = (keep_down + received[2]).astype(jnp.bfloat16)[None]
    return (moe_out, token_grad, gate_grad, up_grad, down_grad)


def solution(mesh):
    placed = (
        P("expert", "replica"),
        P("expert", None),
        P("expert", None),
        P("expert", "replica", None),
        P("expert", "replica", None),
        P("expert", None, "replica"),
        P("expert", "replica"),
    )
    return jax.shard_map(
        per_device,
        mesh=mesh,
        in_specs=placed,
        out_specs=(
            P("expert", "replica"),
            P("expert", "replica"),
            P("expert", "replica", None),
            P("expert", "replica", None),
            P("expert", None, "replica"),
        ),
        check_vma=False,
    )
```

profile of v0, /device:TPU:1, one launch (start us, length us, event | category | flops | bytes accessed | tf_op | source)
XLA Modules:
  0.0 322.7 jit_solution(3056633494185465903)
XLA Ops:
  0.7 8.9 %collective-permute-start.2 = (bf16[512,448]{0,1:T(8,128)(2,1)}, bf16[512,448]{0,1:T(8,128)(2,1)S(1)}, u32[]{:S(2)}, u32[]{:S(2)}) collective-permute-start(bf16[512,448]{0,1:T(8,128)(2,1)} %bitcast.169), channel_id=1, source_target_pairs={{0,8},{8,0},{16,24},{24,16},{32,40},{40,32},{48,56},{56,48},{64,72... | collective-permute-start | bytes 1376264 | tf_op jit(solution)/shard_map/ppermute | solution.py:14
  13.7 1.2 gather_fusion.2
  15.9 8.1 %all-to-all-start.2 = ((bf16[64,2,448]{2,1,0:T(2,128)(2,1)}), bf16[64,2,448]{2,1,0:T(2,128)(2,1)S(1)}, u32[]{:S(2)}, u32[]{:S(2)}) async-start(bf16[64,2,448]{2,1,0:T(2,128)(2,1)} %select_convert_fusion.3), calls=%async_computation.2 | async-start | bytes 262144 | tf_op jit(solution)/shard_map/all_to_all | solution.py:63
  24.0 2.4 collective-permute-start.1
  26.4 2.0 collective-permute-start
  30.4 4.0 %all-to-all-done.2 = bf16[64,2,448]{2,1,0:T(2,128)(2,1)S(1)} async-done(((bf16[64,2,448]{2,1,0:T(2,128)(2,1)}), bf16[64,2,448]{2,1,0:T(2,128)(2,1)S(1)}, u32[]{:S(2)}, u32[]{:S(2)}) %all-to-all-start.2) | async-done | bytes 114720 | tf_op jit(solution)/shard_map/all_to_all | solution.py:63
  34.4 6.3 %all-to-all-start = ((bf16[64,2,448]{2,1,0:T(2,128)(2,1)}), bf16[64,2,448]{2,1,0:T(2,128)(2,1)S(1)}, u32[]{:S(2)}, u32[]{:S(2)}) async-start(bf16[64,2,448]{2,1,0:T(2,128)(2,1)} %broadcast_select_fusion), calls=%async_computation | async-start | bytes 262144 | tf_op jit(solution)/shard_map/all_to_all | solution.py:56
  41.6 9.5 %all-to-all-done = bf16[64,2,448]{2,1,0:T(2,128)(2,1)S(1)} async-done(((bf16[64,2,448]{2,1,0:T(2,128)(2,1)}), bf16[64,2,448]{2,1,0:T(2,128)(2,1)S(1)}, u32[]{:S(2)}, u32[]{:S(2)}) %all-to-all-start) | async-done | bytes 114720 | tf_op jit(solution)/shard_map/all_to_all | solution.py:56
  51.3 24.1 %all_gather.17 = bf16[128,3584]{0,1:T(8,128)(2,1)} all-gather(bf16[128,448]{0,1:T(8,128)(2,1)S(1)} %copy.62), channel_id=1, replica_groups=mesh['expert'=64,'replica'=8] {'replica'}, dimensions={1}, use_global_device_ids=true | all-gather | bytes 1032192 | tf_op jit(solution)/shard_map/all_gather | solution.py:115
  75.6 2.1 copy.63
  77.7 6.0 %all-to-all-start.3 = ((bf16[2,512,448]{2,0,1:T(2,128)(2,1)}), bf16[2,512,448]{2,0,1:T(2,128)(2,1)}, u32[]{:S(2)}, u32[]{:S(2)}) async-start(bf16[2,512,448]{2,0,1:T(2,128)(2,1)} %copy.63), calls=%async_computation.3 | async-start | bytes 2097152 | tf_op jit(solution)/shard_map/all_to_all | solution.py:116
  83.7 41.3 %all_gather.15 = bf16[128,3584]{0,1:T(8,128)(2,1)S(1)} all-gather(bf16[128,448]{0,1:T(8,128)(2,1)S(1)} %copy.57), channel_id=1, replica_groups=mesh['expert'=64,'replica'=8] {'replica'}, dimensions={1}, use_global_device_ids=true | all-gather | bytes 1032192 | tf_op jit(solution)/shard_map/all_gather | solution.py:80
  125.0 1.1 select_bitcast_fusion.3
  127.0 1.0 pad_maximum_fusion.2
  128.0 4.3 %copy.69 = bf16[2,64,3584]{1,0,2:T(2,128)(2,1)S(1)} copy(bf16[2,64,3584]{2,1,0:T(8,128)(2,1)} %pad_maximum_fusion.2) | data formatting | bytes 1835008 | tf_op jit(solution)/shard_map/stack | solution.py:20
  132.3 2.1 reshape.363
  134.4 4.2 %all-to-all-start.5 = ((bf16[8,2,28672]{2,1,0:T(2,128)(2,1)}), bf16[8,2,28672]{2,1,0:T(2,128)(2,1)}, u32[]{:S(2)}, u32[]{:S(2)}) async-start(bf16[8,2,28672]{2,1,0:T(2,128)(2,1)} %reshape.363), calls=%async_computation.5 | async-start | bytes 1835008 | tf_op jit(solution)/shard_map/all_to_all | solution.py:130
  138.7 1.2 select_bitcast_fusion.5
  140.8 1.0 pad_maximum_fusion.1
  141.9 4.3 %copy.66 = bf16[2,64,3584]{1,0,2:T(2,128)(2,1)S(1)} copy(bf16[2,64,3584]{2,1,0:T(8,128)(2,1)} %pad_maximum_fusion.1) | data formatting | bytes 1835008 | tf_op jit(solution)/shard_map/stack | solution.py:20
  146.1 2.1 reshape.365
  148.3 2.2 fusion.9
  150.4 1.4 copy.64
  152.4 2.1 all_to_all.57
  154.5 6.7 %all-to-all-start.4 = ((bf16[8,2,28672]{2,1,0:T(2,128)(2,1)}), bf16[8,2,28672]{2,1,0:T(2,128)(2,1)}, u32[]{:S(2)}, u32[]{:S(2)}) async-start(bf16[8,2,28672]{2,1,0:T(2,128)(2,1)} %reshape.365), calls=%async_computation.4 | async-start | bytes 1835008 | tf_op jit(solution)/shard_map/all_to_all | solution.py:129
  162.8 30.9 %all_gather.16 = bf16[128,2,512]{0,2,1:T(8,128)(2,1)S(1)} all-gather(bf16[128,2,64]{0,2,1:T(8,128)(2,1)S(1)} %get-tuple-element.61), channel_id=1, replica_groups=mesh['expert'=64,'replica'=8] {'replica'}, dimensions={2}, use_global_device_ids=true | all-gather | bytes 294912 | tf_op jit(solution)/shard_map/all_gather | solution.py:98
  195.1 4.5 %reshape.364 = bf16[3584,2,64]{2,1,0:T(2,128)(2,1)S(1)} reshape(bf16[8,2,28672]{2,1,0:T(2,128)(2,1)} %all-to-all-done.5) | data formatting | bytes 1835008
  199.6 3.5 %copy.70 = bf16[2,64,8,448]{3,1,2,0:T(8,128)(2,1)} copy(bf16[2,64,8,448]{1,0,3,2:T(2,128)(2,1)S(1)} %bitcast.164) | data formatting | bytes 1835008 | tf_op jit(solution)/shard_map/all_to_all | solution.py:130
  203.1 18.4 %all_gather.19 = bf16[128,2,512]{0,2,1:T(8,128)(2,1)S(1)} all-gather(bf16[128,2,64]{0,2,1:T(8,128)(2,1)S(1)} %get-tuple-element.60), channel_id=1, replica_groups=mesh['expert'=64,'replica'=8] {'replica'}, dimensions={2}, use_global_device_ids=true | all-gather | bytes 294912 | tf_op jit(solution)/shard_map/all_gather | solution.py:126
  221.5 18.8 %all_gather.18 = bf16[128,2,512]{0,2,1:T(8,128)(2,1)S(1)} all-gather(bf16[128,2,64]{0,2,1:T(8,128)(2,1)S(1)} %get-tuple-element.59), channel_id=1, replica_groups=mesh['expert'=64,'replica'=8] {'replica'}, dimensions={2}, use_global_device_ids=true | all-gather | bytes 294912 | tf_op jit(solution)/shard_map/all_gather | solution.py:125
  240.3 1.7 fusion.7
  242.3 27.9 %all-to-all-start.1 = ((bf16[64,2,448]{2,1,0:T(2,128)(2,1)}), bf16[64,2,448]{2,1,0:T(2,128)(2,1)S(1)}, u32[]{:S(2)}, u32[]{:S(2)}) async-start(bf16[64,2,448]{2,1,0:T(2,128)(2,1)} %reshape.212), calls=%async_computation.1 | async-start | bytes 262144 | tf_op jit(solution)/shard_map/all_to_all | solution.py:103
  270.2 5.3 %reshape.366 = bf16[3584,2,64]{2,1,0:T(2,128)(2,1)} reshape(bf16[8,2,28672]{2,1,0:T(2,128)(2,1)} %all-to-all-done.4) | data formatting | bytes 1835008
  275.5 5.8 %copy.67 = bf16[2,64,8,448]{3,1,2,0:T(8,128)(2,1)} copy(bf16[2,64,8,448]{1,0,3,2:T(2,128)(2,1)} %bitcast.165) | data formatting | bytes 1835008 | tf_op jit(solution)/shard_map/all_to_all | solution.py:129
  281.3 1.8 convolution_bitcast_fusion.1
  284.6 2.3 select_convert_fusion.2
  286.9 2.4 collective-permute-start.3
  289.3 2.0 collective-permute-start.4
  291.3 1.7 fusion.16
  293.0 10.3 %all-to-all-start.6 = ((bf16[64,2,448]{2,1,0:T(2,128)(2,1)}), bf16[64,2,448]{2,1,0:T(2,128)(2,1)S(1)}, u32[]{:S(2)}, u32[]{:S(2)}) async-start(bf16[64,2,448]{2,1,0:T(2,128)(2,1)} %reshape.216), calls=%async_computation.6 | async-start | bytes 262144 | tf_op jit(solution)/shard_map/all_to_all | solution.py:138
  303.3 1.5 select_convert_fusion
  304.8 2.4 collective-permute-start.5
  307.3 0.9 gather_fusion.1
  308.2 5.4 %all-to-all-done.6 = bf16[64,2,448]{2,1,0:T(2,128)(2,1)S(1)} async-done(((bf16[64,2,448]{2,1,0:T(2,128)(2,1)}), bf16[64,2,448]{2,1,0:T(2,128)(2,1)S(1)}, u32[]{:S(2)}, u32[]{:S(2)}) %all-to-all-start.6) | async-done | bytes 114720 | tf_op jit(solution)/shard_map/all_to_all | solution.py:138
  313.8 0.9 gather_fusion.4
  316.1 2.5 fusion.13
  318.6 2.0 fusion.14
  320.6 2.1 fusion.15
  (100 shorter events, 17.1 us)
Async XLA Ops:
  0.6 10.5 %copy-start = (bf16[12,448]{1,0:T(8,128)(2,1)S(1)}, bf16[12,448]{1,0:T(8,128)(2,1)}, u32[]{:S(2)}) copy-start(bf16[12,448]{1,0:T(8,128)(2,1)} %param.21) | copy-start | bytes 32260
  0.6 27.7 %copy-start.20 = (s32[12,8]{0,1:T(8,128)S(1)}, s32[12,8]{0,1:T(8,128)}, u32[]{:S(2)}) copy-start(s32[12,8]{0,1:T(8,128)} %param.16) | copy-start | bytes 1156
  0.7 23.4 %copy-start.17 = (bf16[1,64,3584]{2,1,0:T(8,128)(2,1)S(1)}, bf16[1,64,3584]{2,1,0:T(8,128)(2,1)}, u32[]{:S(2)}) copy-start(bf16[1,64,3584]{2,1,0:T(8,128)(2,1)} %param.19) | copy-start | bytes 1376260
  0.7 27.7 %copy-start.1 = (bf16[12,448]{1,0:T(8,128)(2,1)S(1)}, bf16[12,448]{1,0:T(8,128)(2,1)}, u32[]{:S(2)}) copy-start(bf16[12,448]{1,0:T(8,128)(2,1)} %param.15) | copy-start | bytes 32260
  0.7 74.7 %collective-permute-start.2 = (bf16[512,448]{0,1:T(8,128)(2,1)}, bf16[512,448]{0,1:T(8,128)(2,1)S(1)}, u32[]{:S(2)}, u32[]{:S(2)}) collective-permute-start(bf16[512,448]{0,1:T(8,128)(2,1)} %bitcast.169), channel_id=1, source_target_pairs={{0,8},{8,0},{16,24},{24,16},{32,40},{40,32},{48,56},{56,48},{64,72... | collective-permute-start | bytes 1376264 | tf_op jit(solution)/shard_map/ppermute | solution.py:14
  13.1 0.6 copy-start.18
  15.9 18.4 %all-to-all-start.2 = ((bf16[64,2,448]{2,1,0:T(2,128)(2,1)}), bf16[64,2,448]{2,1,0:T(2,128)(2,1)S(1)}, u32[]{:S(2)}, u32[]{:S(2)}) async-start(bf16[64,2,448]{2,1,0:T(2,128)(2,1)} %select_convert_fusion.3), calls=%async_computation.2 | async-start | bytes 262144 | tf_op jit(solution)/shard_map/all_to_all | solution.py:63
  24.0 101.0 %collective-permute-start.1 = (bf16[64,3584]{1,0:T(8,128)(2,1)S(1)}, bf16[64,3584]{1,0:T(8,128)(2,1)}, u32[]{:S(2)}, u32[]{:S(2)}) collective-permute-start(bf16[64,3584]{1,0:T(8,128)(2,1)S(1)} %bitcast.170), channel_id=1, source_target_pairs={{0,8},{8,0},{16,24},{24,16},{32,40},{40,32},{48,56},{56,48},{64,72... | collective-permute-start | bytes 1376264 | tf_op jit(solution)/shard_map/ppermute | solution.py:14
  26.4 112.3 %collective-permute-start = (bf16[64,3584]{1,0:T(8,128)(2,1)}, bf16[64,3584]{1,0:T(8,128)(2,1)}, u32[]{:S(2)}, u32[]{:S(2)}) collective-permute-start(bf16[64,3584]{1,0:T(8,128)(2,1)} %bitcast.3), channel_id=1, source_target_pairs={{0,8},{8,0},{16,24},{24,16},{32,40},{40,32},{48,56},{56,48},{64,72... | collective-permute-start | bytes 1376264 | tf_op jit(solution)/shard_map/ppermute | solution.py:14
  28.4 47.0 %copy-start.16 = (bf16[1,512,448]{1,2,0:T(8,128)(2,1)S(1)}, bf16[1,512,448]{1,2,0:T(8,128)(2,1)}, u32[]{:S(2)}) copy-start(bf16[1,512,448]{1,2,0:T(8,128)(2,1)} %param.20) | copy-start | bytes 1376260
  34.4 16.7 %all-to-all-start = ((bf16[64,2,448]{2,1,0:T(2,128)(2,1)}), bf16[64,2,448]{2,1,0:T(2,128)(2,1)S(1)}, u32[]{:S(2)}, u32[]{:S(2)}) async-start(bf16[64,2,448]{2,1,0:T(2,128)(2,1)} %broadcast_select_fusion), calls=%async_computation | async-start | bytes 262144 | tf_op jit(solution)/shard_map/all_to_all | solution.py:56
  75.5 2.2 copy-start.6
  77.7 56.7 %all-to-all-start.3 = ((bf16[2,512,448]{2,0,1:T(2,128)(2,1)}), bf16[2,512,448]{2,0,1:T(2,128)(2,1)}, u32[]{:S(2)}, u32[]{:S(2)}) async-start(bf16[2,512,448]{2,0,1:T(2,128)(2,1)} %copy.63), calls=%async_computation.3 | async-start | bytes 2097152 | tf_op jit(solution)/shard_map/all_to_all | solution.py:116
  126.1 0.8 copy-start.12
  126.1 0.9 copy-start.13
  134.4 20.1 %all-to-all-start.5 = ((bf16[8,2,28672]{2,1,0:T(2,128)(2,1)}), bf16[8,2,28672]{2,1,0:T(2,128)(2,1)}, u32[]{:S(2)}, u32[]{:S(2)}) async-start(bf16[8,2,28672]{2,1,0:T(2,128)(2,1)} %reshape.363), calls=%async_computation.5 | async-start | bytes 1835008 | tf_op jit(solution)/shard_map/all_to_all | solution.py:130
  139.9 0.8 copy-start.8
  139.9 0.9 copy-start.10
  152.4 8.8 %copy-start.4 = (bf16[128,3584]{0,1:T(8,128)(2,1)S(1)}, bf16[128,3584]{0,1:T(8,128)(2,1)}, u32[]{:S(2)}) copy-start(bf16[128,3584]{0,1:T(8,128)(2,1)} %all_gather.17) | copy-start | bytes 2752516
  154.5 6.7 %copy-start.5 = (bf16[2,64,3584]{2,1,0:T(8,128)(2,1)S(1)}, bf16[2,64,3584]{2,1,0:T(8,128)(2,1)}, u32[]{:S(2)}) copy-start(bf16[2,64,3584]{2,1,0:T(8,128)(2,1)} %all_to_all.57) | copy-start | bytes 2752516
  154.5 7.1 %copy-start.21 = (f32[128,2,64]{0,2,1:T(8,128)S(1)}, f32[128,2,64]{0,2,1:T(8,128)}, u32[]{:S(2)}) copy-start(f32[128,2,64]{0,2,1:T(8,128)} %fusion.9) | copy-start | bytes 196612
  154.5 87.8 %all-to-all-start.4 = ((bf16[8,2,28672]{2,1,0:T(2,128)(2,1)}), bf16[8,2,28672]{2,1,0:T(2,128)(2,1)}, u32[]{:S(2)}, u32[]{:S(2)}) async-start(bf16[8,2,28672]{2,1,0:T(2,128)(2,1)} %reshape.365), calls=%async_computation.4 | async-start | bytes 1835008 | tf_op jit(solution)/shard_map/all_to_all | solution.py:129
  161.2 1.0 copy-start.9
  161.2 1.1 copy-start.11
  162.3 31.3 %copy-start.7 = (bf16[1,512,448]{1,2,0:T(8,128)(2,1)S(1)}, bf16[1,512,448]{1,2,0:T(8,128)(2,1)}, u32[]{:S(2)}) copy-start(bf16[1,512,448]{1,2,0:T(8,128)(2,1)} %copy-done.6) | copy-start | bytes 1376260
  193.6 0.7 copy-start.14
  242.3 50.6 %all-to-all-start.1 = ((bf16[64,2,448]{2,1,0:T(2,128)(2,1)}), bf16[64,2,448]{2,1,0:T(2,128)(2,1)S(1)}, u32[]{:S(2)}, u32[]{:S(2)}) async-start(bf16[64,2,448]{2,1,0:T(2,128)(2,1)} %reshape.212), calls=%async_computation.1 | async-start | bytes 262144 | tf_op jit(solution)/shard_map/all_to_all | solution.py:103
  281.3 1.8 copy-start.3
  283.7 7.6 %copy-start.15 = (bf16[128,2,512]{0,2,1:T(8,128)(2,1)S(1)}, bf16[128,2,512]{0,2,1:T(8,128)(2,1)}, u32[]{:S(2)}) copy-start(bf16[128,2,512]{0,2,1:T(8,128)(2,1)} %copy-done.14) | copy-start | bytes 786436
  286.9 29.2 %collective-permute-start.3 = (bf16[64,3584]{1,0:T(8,128)(2,1)}, bf16[64,3584]{1,0:T(8,128)(2,1)}, u32[]{:S(2)}, u32[]{:S(2)}) collective-permute-start(bf16[64,3584]{1,0:T(8,128)(2,1)} %select_convert_fusion.2), channel_id=1, source_target_pairs={{0,8},{8,0},{16,24},{24,16},{32,40},{40,32},{48,56},{56,48},{64,72... | collective-permute-start | bytes 1376264 | tf_op jit(solution)/shard_map/ppermute | solution.py:14
  289.3 29.2 %collective-permute-start.4 = (bf16[64,3584]{1,0:T(8,128)(2,1)S(1)}, bf16[64,3584]{1,0:T(8,128)(2,1)}, u32[]{:S(2)}, u32[]{:S(2)}) collective-permute-start(bf16[64,3584]{1,0:T(8,128)(2,1)S(1)} %select_convert_fusion.1), channel_id=1, source_target_pairs={{0,8},{8,0},{16,24},{24,16},{32,40},{40,32},{48,56},{56,48},{64,72... | collective-permute-start | bytes 1376264 | tf_op jit(solution)/shard_map/ppermute | solution.py:14
  293.0 20.7 %all-to-all-start.6 = ((bf16[64,2,448]{2,1,0:T(2,128)(2,1)}), bf16[64,2,448]{2,1,0:T(2,128)(2,1)S(1)}, u32[]{:S(2)}, u32[]{:S(2)}) async-start(bf16[64,2,448]{2,1,0:T(2,128)(2,1)} %reshape.216), calls=%async_computation.6 | async-start | bytes 262144 | tf_op jit(solution)/shard_map/all_to_all | solution.py:138
  303.3 12.1 %copy-start.19 = (f32[12,8]{1,0:T(8,128)S(1)}, f32[12,8]{1,0:T(8,128)}, u32[]{:S(2)}) copy-start(f32[12,8]{1,0:T(8,128)} %copy-done.18) | copy-start | bytes 1156
  304.8 15.7 %collective-permute-start.5 = (bf16[512,448]{0,1:T(8,128)(2,1)S(1)}, bf16[512,448]{0,1:T(8,128)(2,1)}, u32[]{:S(2)}, u32[]{:S(2)}) collective-permute-start(bf16[512,448]{0,1:T(8,128)(2,1)S(1)} %select_convert_fusion), channel_id=1, source_target_pairs={{0,8},{8,0},{16,24},{24,16},{32,40},{40,32},{48,56},{56,48},{64,72... | collective-permute-start | bytes 1376264 | tf_op jit(solution)/shard_map/ppermute | solution.py:14
  318.6 2.0 copy-start.2
where the time goes:
time: 324 us; the launch traced here: 323 us
  blocking collectives  133 us (41%)
  starting transfers between devices  89.4 us (28%)
  local copies, waits for them, and re-layouts  50.9 us (16%)
  other arithmetic  19.4 us (6%)
  waiting for transfers between devices  18.9 us (6%)
  matrix products  9.43 us (3%)
    all_gather x1, blocking collectives, per_device(): full_rows = lax.all_gather(rows_part, 'replica', axis=1, tiled=True)  41.3 us
    all_gather x1, blocking collectives, per_device(): lax.all_gather(hidden, 'replica', axis=2, tiled=True)  30.9 us
    all_to_all x1, starting transfers between devices, per_device(): lax.all_to_all(expert_out.reshape(experts_axis, capacity, slice_width), '...  27.9 us
    all_gather x1, blocking collectives, per_device(): full_grads = lax.all_gather(grads_part, 'replica', axis=1, tiled=True)  24.1 us
    ppermute x6, starting transfers between devices, partner_2(): return lax.ppermute(block, axis, route)  19.9 us
    unnamed x50, local copies, waits for them, and re-layouts  18.8 us
    all_gather x1, blocking collectives, per_device(): lax.all_gather(gate_act, 'replica', axis=2, tiled=True)  18.8 us
    all_gather x1, blocking collectives, per_device(): lax.all_gather(up_act, 'replica', axis=2, tiled=True)  18.4 us
  transfers between devices with their start and end apart: 13, of which 3 were waited for; matrix products, arithmetic and copies ran while one was open for 22% of the time, Pallas kernels for 0%

commit v1 on v0

v1 whole, which is shorter than its diff:
```python
import functools

import jax
import jax.numpy as jnp
from jax import lax
from jax.experimental import pallas as pl
from jax.experimental.pallas import tpu as pltpu
from jax.sharding import PartitionSpec as P

MESH = pl.DeviceIdType.MESH
F32 = jnp.float32
BF16 = jnp.bfloat16
NN = (((1,), (0,)), ((), ()))
NT = (((1,), (1,)), ((), ()))
TN = (((0,), (0,)), ((), ()))


def mm(a, b, dims=NN):
    return lax.dot_general(a, b, dims, preferred_element_type=F32)


def split2(v):
    hi = v.astype(BF16)
    return hi, (v - hi.astype(F32)).astype(BF16)


def log2(n):
    return n.bit_length() - 1


def transposer(rows, outer, inner):
    r = lax.broadcasted_iota(jnp.int32, (rows, rows), 0)
    q = lax.broadcasted_iota(jnp.int32, (rows, rows), 1)
    hi = r >> (1 + log2(inner))
    lo = (r >> 1) & (inner - 1)
    want = (lo << (1 + log2(outer))) + (hi << 1) + (r & 1)
    return jnp.where(q == want, 1.0, 0.0).astype(BF16)


def kernel(
    nz,
    nd,
    ny,
    tok_ref,
    ids_ref,
    gv_ref,
    wg_ref,
    wu_ref,
    wd_ref,
    og_ref,
    moe_ref,
    tg_ref,
    gg_ref,
    ug_ref,
    dg_ref,
    tok16,
    og16,
    ids16,
    gv16,
    a_send,
    a_recv,
    b_send,
    dy_buf,
    x_all,
    w_raw,
    w_blk,
    wd_all,
    acc,
    dh_send,
    dh_recv,
    h_cat,
    rs_send,
    rs_recv,
    ret_send,
    ret_mid,
    ret_fwd,
    ret_recv,
    give,
    got,
    keep,
    give_d,
    got_d,
    keep_d,
    send_sem,
    recv_sem,
    local_sem,
):
    toks, top = ids_ref.shape
    feat = tok_ref.shape[1]
    hid = wg_ref.shape[0]
    rows = 2 * nz * nd
    half_rows = rows // 2
    hs = ny // 2
    me = lax.axis_index("expert")
    y = lax.axis_index("replica")
    c = lax.rem(me, 2)
    z = lax.rem(me // 2, nz)
    x = me // (2 * nz)
    d = 2 * x + c

    def at_z(k):
        t = lax.rem(z + k, nz)
        return t, {"expert": (x * nz + t) * 2 + c}

    def at_d(k):
        t = lax.rem(d + k, nd)
        return t, {"expert": ((t // 2) * nz + z) * 2 + lax.rem(t, 2)}

    def at_y(k):
        t = lax.rem(y + k + ny, ny)
        return t, {"replica": t}

    other = {"expert": (x * nz + z) * 2 + 1 - c}
    _, right = at_y(1)
    _, left = at_y(-1)

    used = []

    def remote(src, dst, dev):
        n = len(used)
        copy = pltpu.make_async_remote_copy(
            src_ref=src,
            dst_ref=dst,
            send_sem=send_sem.at[n],
            recv_sem=recv_sem.at[n],
            device_id=dev,
            device_id_type=MESH,
        )
        copy.start()
        used.append(copy)
        return copy

    barrier = pltpu.get_barrier_semaphore()
    partners = (
        [at_z(k)[1] for k in range(1, nz)]
        + [at_d(k)[1] for k in range(1, nd)]
        + [at_y(k)[1] for k in range(1, ny)]
    )
    for dev in partners:
        pl.semaphore_signal(barrier, inc=1, device_id=dev, device_id_type=MESH)

    own = [
        pltpu.make_async_copy(wd_ref, wd_all.at[:, 0:hid], local_sem.at[0]),
        pltpu.make_async_copy(wg_ref, w_raw.at[0], local_sem.at[1]),
        pltpu.make_async_copy(wu_ref, w_raw.at[2], local_sem.at[2]),
    ]
    for copy in own:
        copy.start()

    tok16[...] = jnp.zeros_like(tok16)
    og16[...] = jnp.zeros_like(og16)
    ids16[...] = jnp.full_like(ids16, -1)
    gv16[...] = jnp.zeros_like(gv16)
    tok16[0:toks, :] = tok_ref[...]
    og16[0:toks, :] = og_ref[...]
    ids16[0:toks, :] = ids_ref[...]
    gv16[0:toks, :] = gv_ref[...]
    lane = lax.broadcasted_iota(jnp.int32, (16, rows), 1)
    dd = (lane >> 1) & (nd - 1)
    expert = ((dd >> 1) << log2(nz)) + (lane >> (1 + log2(nd)))
    rank = (lane & 3).astype(F32)
    named = jnp.zeros((16, rows), F32)
    gates = jnp.zeros((16, rows), F32)
    for k in range(top):
        hit = ids16[:, k : k + 1] == expert
        named = jnp.where(hit, 1.0, named)
        gates = jnp.where(hit, gv16[:, k : k + 1], gates)
    t_row = lax.broadcasted_iota(jnp.int32, (16, 16), 0)
    t_col = lax.broadcasted_iota(jnp.int32, (16, 16), 1)
    before = jnp.where(t_col < t_row, 1.0, 0.0).astype(BF16)
    ahead = mm(before, named.astype(BF16))
    chosen = jnp.where(ahead == rank, named, 0.0)
    pick = chosen.astype(BF16)
    gate_hi, gate_lo = split2(gates * chosen)

    rows_x = mm(pick, tok16[...], TN).astype(BF16)
    a_send[0] = rows_x.reshape(nz, 2 * nd, feat)
    pl.semaphore_wait(barrier, len(partners))

    def stage_a(n):
        copies = []
        for k in range(1, nz):
            t, dev = at_z(k)
            copies.append(remote(a_send.at[n, t], a_recv.at[n, z], dev))
        a_recv[n, z] = a_send[n, z]
        return copies

    def stage_b(n, copies, dst):
        for copy in copies:
            copy.wait_recv()
        sorted_rows = mm(transposer(rows, nd, nz), a_recv[n].reshape(rows, feat))
        b_send[n] = sorted_rows.astype(BF16).reshape(nd, 2 * nz, feat)
        out = []
        for k in range(1, nd):
            t, dev = at_d(k)
            out.append(remote(b_send.at[n, t], dst.at[d], dev))
        dst[d] = b_send[n, d]
        return out

    a_x = stage_a(0)
    rows_dy = (mm(gate_hi, og16[...], TN) + mm(gate_lo, og16[...], TN)).astype(BF16)
    a_send[1] = rows_dy.reshape(nz, 2 * nd, feat)
    a_dy = stage_a(1)
    peer_d = remote(wd_ref, wd_all.at[:, hid : 2 * hid], other)
    peer_g = remote(wg_ref, w_raw.at[1], other)
    peer_u = remote(wu_ref, w_raw.at[3], other)

    def cut(j):
        for b in range(ny):
            w_blk[b, j * hid : (j + 1) * hid, :] = w_raw[j, :, b * feat : (b + 1) * feat]

    own[1].wait()
    cut(0)
    own[2].wait()
    cut(2)
    b_x = stage_b(0, a_x, x_all.at[y])
    b_dy = stage_b(1, a_dy, dy_buf)

    for copy in b_x:
        copy.wait_recv()
    nh = nd // 2

    def ring_send(s):
        br, bl = lax.rem(y - s + ny, ny), lax.rem(y + s, ny)
        if s < hs - 1:
            return remote(x_all.at[br], x_all.at[br], right), remote(
                x_all.at[bl], x_all.at[bl], left
            )
        return remote(x_all.at[br, 0:nh], x_all.at[br, 0:nh], right), remote(
            x_all.at[bl, nh:nd], x_all.at[bl, nh:nd], left
        )

    def rows_of(b):
        return x_all[b].reshape(rows, feat)

    ring = ring_send(0)

    for copy in b_dy:
        copy.wait_recv()
    own[0].wait()
    peer_d.wait_recv()
    dy = dy_buf[...].reshape(rows, feat)
    dh_copies = []
    for k in range(1, ny):
        t, dev = at_y(k)
        dh_send[t] = mm(dy, wd_all[t], NT).astype(BF16)
        dh_copies.append(remote(dh_send.at[t], dh_recv.at[y], dev))
    dh_own = mm(dy, wd_all[y], NT)

    peer_g.wait_recv()
    cut(1)
    peer_u.wait_recv()
    cut(3)
    acc[...] = mm(rows_of(y), w_blk[y], NT)
    for s in range(hs):
        for copy in ring:
            copy.wait_recv()
        if s + 1 < hs:
            ring = ring_send(s + 1)
            for b in (lax.rem(y - 1 - s + ny, ny), lax.rem(y + 1 + s, ny)):
                acc[...] += mm(rows_of(b), w_blk[b], NT)
        else:
            b = lax.rem(y + hs, ny)
            acc[...] += mm(rows_of(b), w_blk[b], NT)

    a = acc[:, 0 : 2 * hid]
    b = acc[:, 2 * hid : 4 * hid]
    sigma = 1.0 / (1.0 + jnp.exp(-a))
    act = a * sigma
    slope = sigma * (1.0 + a * (1.0 - sigma))
    span = pl.ds(pl.multiple_of(y * 2 * hid, 2 * hid), 2 * hid)
    h_cat[:, span] = (act * b).astype(BF16)
    h_copies = []
    for k in range(1, ny):
        _, dev = at_y(k)
        h_copies.append(remote(h_cat.at[:, span], h_cat.at[:, span], dev))
    dh = dh_own
    for k in range(1, ny):
        dh_copies[k - 1].wait_recv()
        dh = dh + dh_recv[lax.rem(y - k + ny, ny)].astype(F32)
    dab = jnp.concatenate(
        [(dh * b * slope).astype(BF16), (dh * act).astype(BF16)], axis=1
    )

    def part(b):
        return mm(dab, w_blk[lax.rem(b + 2 * ny, ny)])

    top_half, low_half = slice(0, half_rows), slice(half_rows, rows)

    def rs_start():
        p = part(y + hs).astype(BF16)
        rs_send[0, 0, top_half] = p[top_half]
        rs_send[1, 0, low_half] = p[low_half]
        return [
            remote(rs_send.at[0, 0, top_half], rs_recv.at[0, 0, top_half], right),
            remote(rs_send.at[1, 0, low_half], rs_recv.at[1, 0, low_half], left),
        ]

    def rs_step(s, before):
        after = []
        for way, dev, dest, half in (
            (0, right, y + hs - s, top_half),
            (1, left, y - hs + s, low_half),
        ):
            p = part(dest)
            before[way].wait_recv()
            if s == 1:
                rs_send[way, s] = p.astype(BF16)
                rs_send[way, s, half] = (
                    p[half] + rs_recv[way, 0, half].astype(F32)
                ).astype(BF16)
            else:
                rs_send[way, s] = (p + rs_recv[way, s - 1].astype(F32)).astype(BF16)
            after.append(remote(rs_send.at[way, s], rs_recv.at[way, s], dev))
        return after

    def back_b(n, value):
        ret_send[n] = value.astype(BF16).reshape(nd, 2 * nz, feat)
        out = []
        for k in range(1, nd):
            t, dev = at_d(k)
            out.append(remote(ret_send.at[n, t], ret_mid.at[n, d], dev))
        ret_mid[n, d] = ret_send[n, d]
        return out

    def back_a(n, copies):
        for copy in copies:
            copy.wait_recv()
        sorted_rows = mm(transposer(rows, nz, nd), ret_mid[n].reshape(rows, feat))
        ret_fwd[n] = sorted_rows.astype(BF16).reshape(nz, 2 * nd, feat)
        out = []
        for k in range(1, nz):
            t, dev = at_z(k)
            out.append(remote(ret_fwd.at[n, t], ret_recv.at[n, z], dev))
        ret_recv[n, z] = ret_fwd[n, z]
        return out

    rs = rs_start()
    rs = rs_step(1, rs)
    for copy in h_copies:
        copy.wait_recv()
    out = mm(h_cat[...], wd_all[...].reshape(ny * 2 * hid, feat))
    out_b = back_b(0, out)
    for b in range(ny):
        g = mm(dab, rows_of(b), TN)
        keep[b, 0:hid] = g[0:hid]
        keep[b, hid : 2 * hid] = g[2 * hid : 3 * hid]
        give[b, 0:hid] = g[hid : 2 * hid].astype(BF16)
        give[b, hid : 2 * hid] = g[3 * hid : 4 * hid].astype(BF16)
    give_copy = remote(give, got, other)
    if hs > 2:
        rs = rs_step(2, rs)
    out_a = back_a(0, out_b)
    for b in range(ny):
        g = mm(h_cat[:, b * 2 * hid : (b + 1) * 2 * hid], dy, TN)
        keep_d[b] = g[0:hid]
        give_d[b] = g[hid : 2 * hid].astype(BF16)
    give_d_copy = remote(give_d, got_d, other)
    for s in range(3, hs):
        rs = rs_step(s, rs)
    dx = part(y)
    for copy in rs:
        copy.wait_recv()
    dx = dx + rs_recv[0, hs - 1].astype(F32) + rs_recv[1, hs - 1].astype(F32)
    dx_b = back_b(1, dx)

    give_copy.wait_recv()
    for b in range(ny):
        span_b = slice(b * feat, (b + 1) * feat)
        gg_ref[:, span_b] = (keep[b, 0:hid] + got[b, 0:hid].astype(F32)).astype(BF16)
        ug_ref[:, span_b] = (
            keep[b, hid : 2 * hid] + got[b, hid : 2 * hid].astype(F32)
        ).astype(BF16)
    dx_a = back_a(1, dx_b)
    give_d_copy.wait_recv()
    dg_ref[...] = (keep_d[...] + got_d[...].astype(F32)).astype(BF16)

    for copy in out_a:
        copy.wait_recv()
    back = ret_recv[0].reshape(rows, feat)
    moe_ref[...] = (mm(gate_hi, back) + mm(gate_lo, back))[0:toks].astype(BF16)
    for copy in dx_a:
        copy.wait_recv()
    tg_ref[...] = mm(pick, ret_recv[1].reshape(rows, feat))[0:toks].astype(BF16)
    for copy in used:
        copy.wait_send()


def per_device(nz, tokens, ids, gate_values, gate_weight, up_weight, down_weight, out_grad):
    ne = lax.axis_size("expert")
    ny = lax.axis_size("replica")
    nd = ne // nz
    toks, feat = tokens.shape
    hid, width = gate_weight.shape[1:]
    rows = 2 * ne
    hs = ny // 2
    copies = 4 * (nz - 1) + 4 * (nd - 1) + 3 + 4 * hs + 2 * (ny - 1) + 2
    vmem = pl.BlockSpec(memory_space=pltpu.VMEM)
    hbm = pl.BlockSpec(memory_space=pl.ANY)
    moe, tg, gg, ug, dg = pl.pallas_call(
        functools.partial(kernel, nz, nd, ny),
        out_shape=(
            jax.ShapeDtypeStruct((toks, feat), BF16),
            jax.ShapeDtypeStruct((toks, feat), BF16),
            jax.ShapeDtypeStruct((hid, width), BF16),
            jax.ShapeDtypeStruct((hid, width), BF16),
            jax.ShapeDtypeStruct((ny, hid, feat), BF16),
        ),
        in_specs=[vmem, vmem, vmem, hbm, hbm, hbm, vmem],
        out_specs=(vmem,) * 5,
        scratch_shapes=[
            pltpu.VMEM((16, feat), BF16),
            pltpu.VMEM((16, feat), BF16),
            pltpu.VMEM((16, ids.shape[1]), jnp.int32),
            pltpu.VMEM((16, ids.shape[1]), F32),
            pltpu.VMEM((2, nz, 2 * nd, feat), BF16),
            pltpu.VMEM((2, nz, 2 * nd, feat), BF16),
            pltpu.VMEM((2, nd, 2 * nz, feat), BF16),
            pltpu.VMEM((nd, 2 * nz, feat), BF16),
            pltpu.VMEM((ny, nd, 2 * nz, feat), BF16),
            pltpu.VMEM((4, hid, width), BF16),
            pltpu.VMEM((ny, 4 * hid, feat), BF16),
            pltpu.VMEM((ny, 2 * hid, feat), BF16),
            pltpu.VMEM((rows, 4 * hid), F32),
            pltpu.VMEM((ny, rows, 2 * hid), BF16),
            pltpu.VMEM((ny, rows, 2 * hid), BF16),
            pltpu.VMEM((rows, ny * 2 * hid), BF16),
            pltpu.VMEM((2, hs, rows, feat), BF16),
            pltpu.VMEM((2, hs, rows, feat), BF16),
            pltpu.VMEM((2, nd, 2 * nz, feat), BF16),
            pltpu.VMEM((2, nd, 2 * nz, feat), BF16),
            pltpu.VMEM((2, nz, 2 * nd, feat), BF16),
            pltpu.VMEM((2, nz, 2 * nd, feat), BF16),
            pltpu.VMEM((ny, 2 * hid, feat), BF16),
            pltpu.VMEM((ny, 2 * hid, feat), BF16),
            pltpu.VMEM((ny, 2 * hid, feat), F32),
            pltpu.VMEM((ny, hid, feat), BF16),
            pltpu.VMEM((ny, hid, feat), BF16),
            pltpu.VMEM((ny, hid, feat), F32),
            pltpu.SemaphoreType.DMA((copies,)),
            pltpu.SemaphoreType.DMA((copies,)),
            pltpu.SemaphoreType.DMA((3,)),
        ],
        compiler_params=pltpu.CompilerParams(
            collective_id=0, has_side_effects=True, vmem_limit_bytes=48 * 1024 * 1024
        ),
    )(
        tokens,
        ids,
        gate_values,
        gate_weight[0],
        up_weight[0],
        down_weight[0].reshape(ny, hid, feat),
        out_grad,
    )
    return moe, tg, gg[None], ug[None], dg.reshape(1, ny * hid, feat)


def solution(mesh):
    nz = 8 if mesh.shape["expert"] == 64 else 2
    rows, whole = P("expert", "replica"), P("expert", None)
    units, slices = P("expert", "replica", None), P("expert", None, "replica")
    return jax.shard_map(
        functools.partial(per_device, nz),
        mesh=mesh,
        in_specs=(rows, whole, whole, units, units, slices, rows),
        out_specs=(rows, rows, units, units, slices),
        check_vma=False,
    )
```

time: 324 us -> 90.3 us (0.28)
  blocking collectives: 133 us -> 0 us
  starting transfers between devices: 89.4 us -> 0 us
  Pallas kernels: 0 us -> 82.3 us
  local copies, waits for them, and re-layouts: 50.9 us -> 5.88 us
  other arithmetic: 19.4 us -> 0 us
  waiting for transfers between devices: 18.9 us -> 0 us
  matrix products: 9.43 us -> 0 us
    all_gather x5 -> x0, blocking collectives: 133 us -> none  [the longest x1 41.3 us: per_device(): full_rows = lax.all_gather(rows_part, 'replica', axis=1, tiled=True)]
    pallas_call x0 -> x1, Pallas kernels: none -> 82.3 us  [per_device(): pl.pallas_call(functools.partial(kernel, nz, nd, ny), out_shape=(jax.Shap...]
    all_to_all x7 -> x0, starting transfers between devices: 69.5 us -> none  [the longest x1 27.9 us: per_device(): lax.all_to_all(expert_out.reshape(experts_axis, capacity, slice_width), '...]
    ppermute x6 -> x0, starting transfers between devices: 19.9 us -> none  [partner_2(): return lax.ppermute(block, axis, route)]
    all_to_all x7 -> x0, waiting for transfers between devices: 18.9 us -> none  [the longest x1 9.5 us: per_device(): lax.all_to_all(send_rows.reshape(experts_axis, capacity, slice_width), 'e...]
    all_to_all x5 -> x0, local copies, waits for them, and re-layouts: 13.4 us -> none  [the longest x1 5.85 us: per_device(): lax.all_to_all(w_gate, 'replica', split_axis=2, concat_axis=1, tiled=True)]
    unnamed x50 -> x18, local copies, waits for them, and re-layouts: 18.8 us -> 5.88 us
    another operation x3 -> x0, local copies, waits for them, and re-layouts: 10.7 us -> none  [pair_join(): return jnp.stack([first_part, second_part], axis=stack_axis)]
  transfers between devices with their start and end apart: 13 -> 0, of which waited for: 3 -> 0; matrix products, arithmetic and copies ran while one was open for 22% -> 0% of each run, Pallas kernels for 0% -> 0%
where the time goes in v1:
time: 90.3 us; the launch traced here: 88.9 us
  Pallas kernels  82.3 us (91%)
  local copies, waits for them, and re-layouts  5.88 us (7%)
    pallas_call x1, Pallas kernels, per_device(): pl.pallas_call(functools.partial(kernel, nz, nd, ny), out_shape=(jax.Shap...  82.3 us
    unnamed x18, local copies, waits for them, and re-layouts  5.88 us

profile of v1, /device:TPU:1, one launch (start us, length us, event | category | flops | bytes accessed | tf_op | source)
XLA Modules:
  0.0 88.9 jit_solution(13421795966325324127)
XLA Ops:
  0.6 0.0 copy-start.4
  0.6 0.8 copy.13.ids_ref
  1.4 0.0 copy-done.4
  1.4 0.1 copy.14.gv_ref
  1.5 0.0 copy-start
  1.5 0.0 copy-start.1
  1.5 0.0 copy-start.2
  1.5 0.0 copy-start.3
  1.5 1.3 %copy.12 = bf16[1,512,448]{2,1,0:T(8,128)(2,1)S(1)} copy(bf16[1,512,448]{1,2,0:T(8,128)(2,1)} %param.12) | data formatting | bytes 917504 | tf_op args[5]
  2.8 0.0 copy-done
  2.8 0.0 copy-done.1
  2.8 0.0 copy-done.2
  2.9 0.0 copy-done.3
  2.9 82.3 %shard_map.110 = (bf16[12,448]{1,0:T(8,128)(2,1)S(1)}, bf16[12,448]{1,0:T(8,128)(2,1)S(1)}, bf16[64,3584]{1,0:T(8,128)(2,1)S(1)}, bf16[64,3584]{1,0:T(8,128)(2,1)S(1)}, bf16[8,64,448]{2,1,0:T(8,128)(2,1)S(1)}) custom-call(bf16[12,448]{1,0:T(8,128)(2,1)S(1)} %copy-done.2, s32[12,8]{1,0:T(8,128)S(1)} %copy.13.ids_ref, f32[12,8]{1,0:T(8,128)S(1)} %copy.14.gv_ref, ...), custom_call_target="tpu_custom_call" | custom-call | tf_op jit(solution)/shard_map/pallas_call | solution.py:400
  85.2 1.0 %copy.15 = bf16[1,512,448]{1,2,0:T(8,128)(2,1)} copy(bf16[1,512,448]{2,1,0:T(8,128)(2,1)S(1)} %bitcast.7) | data formatting | bytes 917504
  86.2 0.6 copy.20
  86.8 0.6 copy.21
  87.4 0.8 copy.22
  88.1 0.8 copy.23
Async XLA Ops:
  0.6 0.8 copy-start.4
  1.5 1.3 %copy-start = (bf16[1,64,3584]{2,1,0:T(8,128)(2,1)S(1)}, bf16[1,64,3584]{2,1,0:T(8,128)(2,1)}, u32[]{:S(2)}) copy-start(bf16[1,64,3584]{2,1,0:T(8,128)(2,1)} %param.10) | copy-start | bytes 1376260
  1.5 1.3 %copy-start.1 = (bf16[1,64,3584]{2,1,0:T(8,128)(2,1)S(1)}, bf16[1,64,3584]{2,1,0:T(8,128)(2,1)}, u32[]{:S(2)}) copy-start(bf16[1,64,3584]{2,1,0:T(8,128)(2,1)} %param.11) | copy-start | bytes 1376260
  1.5 1.3 %copy-start.2 = (bf16[12,448]{1,0:T(8,128)(2,1)S(1)}, bf16[12,448]{1,0:T(8,128)(2,1)}, u32[]{:S(2)}) copy-start(bf16[12,448]{1,0:T(8,128)(2,1)} %tok_ref.1) | copy-start | bytes 32260
  1.5 1.3 %copy-start.3 = (bf16[12,448]{1,0:T(8,128)(2,1)S(1)}, bf16[12,448]{1,0:T(8,128)(2,1)}, u32[]{:S(2)}) copy-start(bf16[12,448]{1,0:T(8,128)(2,1)} %og_ref.1) | copy-start | bytes 32260

commit v2 on v1

v2 whole, which is shorter than its diff:
```python
import functools

import jax
import jax.numpy as jnp
from jax import lax
from jax.experimental import pallas as pl
from jax.experimental.pallas import tpu as pltpu
from jax.sharding import PartitionSpec as P

MESH = pl.DeviceIdType.MESH
F32 = jnp.float32
BF16 = jnp.bfloat16
NN = (((1,), (0,)), ((), ()))
NT = (((1,), (1,)), ((), ()))
TN = (((0,), (0,)), ((), ()))


def mm(a, b, dims=NN):
    return lax.dot_general(a, b, dims, preferred_element_type=F32)


def split2(v):
    hi = v.astype(BF16)
    return hi, (v - hi.astype(F32)).astype(BF16)


def log2(n):
    return n.bit_length() - 1


def transposer(rows, outer, inner):
    r = lax.broadcasted_iota(jnp.int32, (rows, rows), 0)
    q = lax.broadcasted_iota(jnp.int32, (rows, rows), 1)
    hi = r >> (1 + log2(inner))
    lo = (r >> 1) & (inner - 1)
    want = (lo << (1 + log2(outer))) + (hi << 1) + (r & 1)
    return jnp.where(q == want, 1.0, 0.0).astype(BF16)


def kernel(
    nz,
    nd,
    ny,
    tok_ref,
    ids_ref,
    gv_ref,
    wg_ref,
    wu_ref,
    wd_ref,
    og_ref,
    moe_out,
    tg_out,
    gg_out,
    ug_out,
    dg_out,
    moe_ref,
    tg_ref,
    gg_ref,
    ug_ref,
    dg_ref,
    tok_in,
    og_in,
    ids_in,
    gv_in,
    tok16,
    og16,
    ids16,
    gv16,
    wd_raw,
    a_send,
    a_recv,
    b_send,
    dy_buf,
    x_all,
    w_raw,
    w_blk,
    wd_all,
    acc,
    dh_send,
    dh_recv,
    h_cat,
    rs_send,
    rs_recv,
    ret_send,
    ret_mid,
    ret_fwd,
    ret_recv,
    give,
    got,
    keep,
    give_d,
    got_d,
    keep_d,
    send_sem,
    recv_sem,
    local_sem,
):
    top, toks = ids_ref.shape
    feat = tok_ref.shape[1]
    hid = wg_ref.shape[0]
    rows = 2 * nz * nd
    half_rows = rows // 2
    hs = ny // 2
    width = 2 * hid
    me = lax.axis_index("expert")
    y = lax.axis_index("replica")
    c = lax.rem(me, 2)
    z = lax.rem(me // 2, nz)
    x = me // (2 * nz)
    d = 2 * x + c

    def at_z(k):
        t = lax.rem(z + k, nz)
        return t, {"expert": (x * nz + t) * 2 + c}

    def at_d(k):
        t = lax.rem(d + k, nd)
        return t, {"expert": ((t // 2) * nz + z) * 2 + lax.rem(t, 2)}

    def at_y(k):
        t = lax.rem(y + k + ny, ny)
        return t, {"replica": t}

    other = {"expert": (x * nz + z) * 2 + 1 - c}
    _, right = at_y(1)
    _, left = at_y(-1)

    used = []

    def remote(src, dst, dev):
        n = len(used)
        copy = pltpu.make_async_remote_copy(
            src_ref=src,
            dst_ref=dst,
            send_sem=send_sem.at[n],
            recv_sem=recv_sem.at[n],
            device_id=dev,
            device_id_type=MESH,
        )
        copy.start()
        used.append(copy)
        return copy

    barrier = pltpu.get_barrier_semaphore()
    partners = (
        [at_z(k)[1] for k in range(1, nz)]
        + [at_d(k)[1] for k in range(1, nd)]
        + [at_y(k)[1] for k in range(1, ny)]
    )
    for dev in partners:
        pl.semaphore_signal(barrier, inc=1, device_id=dev, device_id_type=MESH)

    small = [
        pltpu.make_async_copy(src, dst, local_sem.at[3 + n])
        for n, (src, dst) in enumerate(
            ((ids_ref, ids_in), (tok_ref, tok_in), (gv_ref, gv_in), (og_ref, og_in))
        )
    ]
    own = [
        pltpu.make_async_copy(wd_ref, wd_raw.at[0], local_sem.at[0]),
        pltpu.make_async_copy(wg_ref, w_raw.at[0], local_sem.at[1]),
        pltpu.make_async_copy(wu_ref, w_raw.at[2], local_sem.at[2]),
    ]
    for copy in small + own:
        copy.start()

    tok16[...] = jnp.zeros_like(tok16)
    og16[...] = jnp.zeros_like(og16)
    ids16[...] = jnp.full_like(ids16, -1)
    gv16[...] = jnp.zeros_like(gv16)
    for copy in small:
        copy.wait()
    tok16[0:toks, :] = tok_in[...]
    og16[0:toks, :] = og_in[...]
    ids16[:, 0:toks] = ids_in[...]
    gv16[:, 0:toks] = gv_in[...]
    slot = lax.broadcasted_iota(jnp.int32, (rows, 16), 0)
    dd = (slot >> 1) & (nd - 1)
    expert = ((dd >> 1) << log2(nz)) + (slot >> (1 + log2(nd)))
    rank = (slot & 3).astype(F32)
    named = jnp.zeros((rows, 16), F32)
    gates = jnp.zeros((rows, 16), F32)
    for k in range(top):
        hit = ids16[k : k + 1, :] == expert
        named = jnp.where(hit, 1.0, named)
        gates = jnp.where(hit, gv16[k : k + 1, :], gates)
    t_row = lax.broadcasted_iota(jnp.int32, (16, 16), 0)
    t_col = lax.broadcasted_iota(jnp.int32, (16, 16), 1)
    before = jnp.where(t_row < t_col, 1.0, 0.0).astype(BF16)
    ahead = mm(named.astype(BF16), before)
    chosen = jnp.where(ahead == rank, named, 0.0)
    pick = chosen.astype(BF16)
    gate_hi, gate_lo = split2(gates * chosen)

    rows_x = mm(pick, tok16[...]).astype(BF16)
    a_send[0] = rows_x.reshape(nz, 2 * nd, feat)
    pl.semaphore_wait(barrier, len(partners))

    def stage_a(n):
        copies = []
        for k in range(1, nz):
            t, dev = at_z(k)
            copies.append(remote(a_send.at[n, t], a_recv.at[n, z], dev))
        a_recv[n, z] = a_send[n, z]
        return copies

    def stage_b(n, copies, dst):
        for copy in copies:
            copy.wait_recv()
        sorted_rows = mm(transposer(rows, nd, nz), a_recv[n].reshape(rows, feat))
        b_send[n] = sorted_rows.astype(BF16).reshape(nd, 2 * nz, feat)
        out = []
        for k in range(1, nd):
            t, dev = at_d(k)
            out.append(remote(b_send.at[n, t], dst.at[d], dev))
        dst[d] = b_send[n, d]
        return out

    a_x = stage_a(0)
    rows_dy = (mm(gate_hi, og16[...]) + mm(gate_lo, og16[...])).astype(BF16)
    a_send[1] = rows_dy.reshape(nz, 2 * nd, feat)
    a_dy = stage_a(1)
    peer_d = remote(wd_ref, wd_raw.at[1], other)
    peer_g = remote(wg_ref, w_raw.at[1], other)
    peer_u = remote(wu_ref, w_raw.at[3], other)

    def cut(j):
        for b in range(ny):
            w_blk[b, j * hid : (j + 1) * hid, :] = w_raw[j, :, b * feat : (b + 1) * feat]

    own[1].wait()
    cut(0)
    own[2].wait()
    cut(2)
    b_x = stage_b(0, a_x, x_all.at[y])
    b_dy = stage_b(1, a_dy, dy_buf)

    nh = nd // 2
    chunks = (slice(0, nh), slice(nh, nd))
    ways = ((0, 1), (1, -1))
    arriving = {}

    def ring_send(s, ch, way, sign):
        b = lax.rem(y - sign * s + ny, ny)
        block = x_all.at[b, chunks[ch]]
        arriving[s, ch, way] = remote(block, block, at_y(sign)[1])

    def rows_of(b):
        return x_all[b].reshape(rows, feat)

    def ring_step(s):
        for ch in range(2):
            for way, sign in ways:
                arriving[s - 1, ch, way].wait_recv()
                if s < hs - 1 or ch == way:
                    ring_send(s, ch, way, sign)
        for way, sign in ways:
            b = lax.rem(y - sign * s + ny, ny)
            acc[...] += mm(rows_of(b), w_blk[b], NT)

    top_half, low_half = slice(0, half_rows), slice(half_rows, rows)
    halves = (top_half, low_half)

    def tree_far(part, send, recv):
        far = {}
        p = part(4).astype(BF16)
        for way, sign in ways:
            send[way, 0, halves[way]] = p[halves[way]]
            far[way, 0] = remote(
                send.at[way, 0, halves[way]], recv.at[way, 0, halves[way]], at_y(2 * sign)[1]
            )
        for way, sign in ways:
            send[way, 1] = part(3 * sign).astype(BF16)
            far[way, 1] = remote(send.at[way, 1], recv.at[way, 1], at_y(sign)[1])
        return far

    def tree_near(part, send, recv):
        near = []
        for way, sign in ways:
            send[way, 2] = part(sign).astype(BF16)
            near.append(remote(send.at[way, 2], recv.at[way, 2], at_y(sign)[1]))
        return near

    def tree_mid(part, send, recv, far):
        mid = []
        for way, sign in ways:
            p = part(2 * sign)
            far[way, 1].wait_recv()
            p = p + recv[way, 1].astype(F32)
            far[way, 0].wait_recv()
            half, rest = halves[way], halves[1 - way]
            send[way, 3, half] = (p[half] + recv[way, 0, half].astype(F32)).astype(BF16)
            send[way, 3, rest] = p[rest].astype(BF16)
            mid.append(remote(send.at[way, 3], recv.at[way, 3], at_y(2 * sign)[1]))
        return mid

    def tree_end(part, recv, near, mid):
        total = part(0)
        for way in range(2):
            near[way].wait_recv()
            total = total + recv[way, 2].astype(F32)
        for way in range(2):
            mid[way].wait_recv()
            total = total + recv[way, 3].astype(F32)
        return total

    def lanes(b):
        return pl.ds(pl.multiple_of(b * width, width), width)

    for copy in b_x:
        copy.wait_recv()
    for ch in range(2):
        for way, sign in ways:
            ring_send(0, ch, way, sign)

    own[0].wait()
    peer_d.wait_recv()
    for b in range(ny):
        span = slice(b * hid, (b + 1) * hid)
        wd_all[:, b * width : (b + 1) * width] = jnp.concatenate(
            [wd_raw[0, :, span], wd_raw[1, :, span]], axis=1
        )
    peer_g.wait_recv()
    cut(1)
    peer_u.wait_recv()
    cut(3)
    acc[...] = mm(rows_of(y), w_blk[y], NT)
    ring_step(1)

    for copy in b_dy:
        copy.wait_recv()
    dy = dy_buf[...].reshape(rows, feat)

    def dh_part(k):
        return mm(dy, wd_all[:, lanes(at_y(k)[0])])

    dh_far = tree_far(dh_part, dh_send, dh_recv)
    dh_near = tree_near(dh_part, dh_send, dh_recv)
    ring_step(2)
    dh_mid = tree_mid(dh_part, dh_send, dh_recv, dh_far)
    ring_step(3)
    for way in range(2):
        arriving[hs - 1, way, way].wait_recv()
    opposite = lax.rem(y + hs, ny)
    acc[...] += mm(rows_of(opposite), w_blk[opposite], NT)

    a = acc[:, 0:width]
    b = acc[:, width : 2 * width]
    sigma = 1.0 / (1.0 + jnp.exp(-a))
    act = a * sigma
    slope = sigma * (1.0 + a * (1.0 - sigma))
    h_cat[:, lanes(y)] = (act * b).astype(BF16)
    dh = tree_end(dh_part, dh_recv, dh_near, dh_mid)
    dab = jnp.concatenate(
        [(dh * b * slope).astype(BF16), (dh * act).astype(BF16)], axis=1
    )

    def dx_part(k):
        return mm(dab, w_blk[at_y(k)[0]])

    def h_send(dist, hops, half=None):
        out = []
        for way, sign in ways:
            b = lax.rem(y - sign * dist + ny, ny)
            block = h_cat.at[:, lanes(b)] if half is None else h_cat.at[halves[way], lanes(b)]
            out.append(remote(block, block, at_y(sign * hops)[1]))
        return out

    dx_far = tree_far(dx_part, rs_send, rs_recv)
    h_two = h_send(0, 2)
    h_one = h_send(0, 1)
    dx_near = tree_near(dx_part, rs_send, rs_recv)

    def back_b(n, value):
        ret_send[n] = value.astype(BF16).reshape(nd, 2 * nz, feat)
        out = []
        for k in range(1, nd):
            t, dev = at_d(k)
            out.append(remote(ret_send.at[n, t], ret_mid.at[n, d], dev))
        ret_mid[n, d] = ret_send[n, d]
        return out

    def back_a(n, copies):
        for copy in copies:
            copy.wait_recv()
        sorted_rows = mm(transposer(rows, nz, nd), ret_mid[n].reshape(rows, feat))
        ret_fwd[n] = sorted_rows.astype(BF16).reshape(nz, 2 * nd, feat)
        out = []
        for k in range(1, nz):
            t, dev = at_z(k)
            out.append(remote(ret_fwd.at[n, t], ret_recv.at[n, z], dev))
        ret_recv[n, z] = ret_fwd[n, z]
        return out

    for b in range(ny):
        g = mm(dab, rows_of(b), TN)
        keep[b, 0:hid] = g[0:hid]
        keep[b, hid : 2 * hid] = g[2 * hid : 3 * hid]
        give[b, 0:hid] = g[hid : 2 * hid].astype(BF16)
        give[b, hid : 2 * hid] = g[3 * hid : 4 * hid].astype(BF16)
    give_copy = remote(give, got, other)
    for copy in h_two:
        copy.wait_recv()
    h_three = h_send(2, 1)
    h_four = h_send(2, 2, half=True)
    dx_mid = tree_mid(dx_part, rs_send, rs_recv, dx_far)
    for copy in h_one + h_three + h_four:
        copy.wait_recv()
    out_b = back_b(0, mm(h_cat[...], wd_all[...], NT))
    g = mm(dy, h_cat[...], TN)
    for b in range(ny):
        span = slice(b * hid, (b + 1) * hid)
        keep_d[:, span] = g[:, b * width : b * width + hid]
        give_d[:, span] = g[:, b * width + hid : (b + 1) * width].astype(BF16)
    give_d_copy = remote(give_d, got_d, other)
    dx_b = back_b(1, tree_end(dx_part, rs_recv, dx_near, dx_mid))
    out_a = back_a(0, out_b)

    give_copy.wait_recv()
    for b in range(ny):
        span_b = slice(b * feat, (b + 1) * feat)
        gg_ref[:, span_b] = (keep[b, 0:hid] + got[b, 0:hid].astype(F32)).astype(BF16)
        ug_ref[:, span_b] = (
            keep[b, hid : 2 * hid] + got[b, hid : 2 * hid].astype(F32)
        ).astype(BF16)
    leaving = []

    def leave(src, dst):
        copy = pltpu.make_async_copy(src, dst, local_sem.at[7 + len(leaving)])
        copy.start()
        leaving.append(copy)

    leave(gg_ref, gg_out)
    leave(ug_ref, ug_out)
    dx_a = back_a(1, dx_b)
    give_d_copy.wait_recv()
    dg_ref[...] = (keep_d[...] + got_d[...].astype(F32)).astype(BF16)
    leave(dg_ref, dg_out)

    for copy in out_a:
        copy.wait_recv()
    back = ret_recv[0].reshape(rows, feat)
    moe_ref[...] = (mm(gate_hi, back, TN) + mm(gate_lo, back, TN))[0:toks].astype(BF16)
    leave(moe_ref, moe_out)
    for copy in dx_a:
        copy.wait_recv()
    tg_ref[...] = mm(pick, ret_recv[1].reshape(rows, feat), TN)[0:toks].astype(BF16)
    leave(tg_ref, tg_out)
    for copy in leaving:
        copy.wait()
    for copy in used:
        copy.wait_send()


def write_out(*refs):
    count = len(refs) // 3
    ins, outs, held = refs[:count], refs[count : 2 * count], refs[2 * count : 3 * count]
    sem = refs[-1]
    read = [pltpu.make_async_copy(i, h, sem.at[n]) for n, (i, h) in enumerate(zip(ins, held))]
    write = [
        pltpu.make_async_copy(h, o, sem.at[count + n])
        for n, (h, o) in enumerate(zip(held, outs))
    ]
    for copy in read:
        copy.start()
    for n in range(count):
        read[n].wait()
        write[n].start()
    for copy in write:
        copy.wait()


def per_device(nz, tokens, ids, gate_values, gate_weight, up_weight, down_weight, out_grad):
    ne = lax.axis_size("expert")
    ny = lax.axis_size("replica")
    nd = ne // nz
    toks, feat = tokens.shape
    top = ids.shape[1]
    hid, width = gate_weight.shape[1:]
    rows = 2 * ne
    hs = ny // 2
    copies = 4 * (nz - 1) + 4 * (nd - 1) + 5 + (4 * hs - 2) + 3 * 8
    hbm = pl.BlockSpec(memory_space=pltpu.HBM)
    moe, tg, gg, ug, dg = pl.pallas_call(
        functools.partial(kernel, nz, nd, ny),
        out_shape=(
            jax.ShapeDtypeStruct((toks, feat), BF16),
            jax.ShapeDtypeStruct((toks, feat), BF16),
            jax.ShapeDtypeStruct((hid, width), BF16),
            jax.ShapeDtypeStruct((hid, width), BF16),
            jax.ShapeDtypeStruct((feat, ny * hid), BF16),
        ),
        in_specs=[hbm] * 7,
        out_specs=(hbm,) * 5,
        scratch_shapes=[
            pltpu.VMEM((toks, feat), BF16),
            pltpu.VMEM((toks, feat), BF16),
            pltpu.VMEM((hid, width), BF16),
            pltpu.VMEM((hid, width), BF16),
            pltpu.VMEM((feat, ny * hid), BF16),
            pltpu.VMEM((toks, feat), BF16),
            pltpu.VMEM((toks, feat), BF16),
            pltpu.VMEM((top, toks), jnp.int32),
            pltpu.VMEM((top, toks), F32),
            pltpu.VMEM((16, feat), BF16),
            pltpu.VMEM((16, feat), BF16),
            pltpu.VMEM((top, 16), jnp.int32),
            pltpu.VMEM((top, 16), F32),
            pltpu.VMEM((2, feat, ny * hid), BF16),
            pltpu.VMEM((2, nz, 2 * nd, feat), BF16),
            pltpu.VMEM((2, nz, 2 * nd, feat), BF16),
            pltpu.VMEM((2, nd, 2 * nz, feat), BF16),
            pltpu.VMEM((nd, 2 * nz, feat), BF16),
            pltpu.VMEM((ny, nd, 2 * nz, feat), BF16),
            pltpu.VMEM((4, hid, width), BF16),
            pltpu.VMEM((ny, 4 * hid, feat), BF16),
            pltpu.VMEM((feat, 2 * ny * hid), BF16),
            pltpu.VMEM((rows, 4 * hid), F32),
            pltpu.VMEM((2, 4, rows, 2 * hid), BF16),
            pltpu.VMEM((2, 4, rows, 2 * hid), BF16),
            pltpu.VMEM((rows, ny * 2 * hid), BF16),
            pltpu.VMEM((2, 4, rows, feat), BF16),
            pltpu.VMEM((2, 4, rows, feat), BF16),
            pltpu.VMEM((2, nd, 2 * nz, feat), BF16),
            pltpu.VMEM((2, nd, 2 * nz, feat), BF16),
            pltpu.VMEM((2, nz, 2 * nd, feat), BF16),
            pltpu.VMEM((2, nz, 2 * nd, feat), BF16),
            pltpu.VMEM((ny, 2 * hid, feat), BF16),
            pltpu.VMEM((ny, 2 * hid, feat), BF16),
            pltpu.VMEM((ny, 2 * hid, feat), F32),
            pltpu.VMEM((feat, ny * hid), BF16),
            pltpu.VMEM((feat, ny * hid), BF16),
            pltpu.VMEM((feat, ny * hid), F32),
            pltpu.SemaphoreType.DMA((copies,)),
            pltpu.SemaphoreType.DMA((copies,)),
            pltpu.SemaphoreType.DMA((12,)),
        ],
        compiler_params=pltpu.CompilerParams(
            collective_id=0, has_side_effects=True, vmem_limit_bytes=60 * 1024 * 1024
        ),
    )(
        tokens,
        ids.T,
        gate_values.T,
        gate_weight[0],
        up_weight[0],
        down_weight[0].T,
        out_grad,
    )
    made = (moe, tg, gg, ug, dg)
    moe, tg, gg, ug, dg = pl.pallas_call(
        write_out,
        out_shape=tuple(jax.ShapeDtypeStruct(v.shape, v.dtype) for v in made),
        in_specs=[hbm] * 5,
        out_specs=(hbm,) * 5,
        scratch_shapes=[pltpu.VMEM(v.shape, v.dtype) for v in made]
        + [pltpu.SemaphoreType.DMA((10,))],
    )(*made)
    return moe, tg, gg[None], ug[None], dg.T[None]


def solution(mesh):
    nz = 8 if mesh.shape["expert"] == 64 else 2
    rows, whole = P("expert", "replica"), P("expert", None)
    units, slices = P("expert", "replica", None), P("expert", None, "replica")
    return jax.shard_map(
        functools.partial(per_device, nz),
        mesh=mesh,
        in_specs=(rows, whole, whole, units, units, slices, rows),
        out_specs=(rows, rows, units, units, slices),
        check_vma=False,
    )
```

time: 90.3 us -> 79.9 us (0.88); the launches traced: 88.9 us -> 79.6 us
  local copies, waits for them, and re-layouts: 5.88 us -> 0 us
  Pallas kernels: 82.3 us -> 79 us
    unnamed x18 -> x0, local copies, waits for them, and re-layouts: 5.88 us -> none
    pallas_call x1, Pallas kernels: 82.3 us -> 76.8 us  [per_device(): pl.pallas_call(functools.partial(kernel, nz, nd, ny), out_shape=(jax.Shap...]
    pallas_call x0 -> x1, Pallas kernels: none -> 2.21 us  [per_device(): pl.pallas_call(write_out, out_shape=tuple((jax.ShapeDtypeStruct(v.shape,...]
where the time goes in v2:
time: 79.9 us; the launch traced here: 79.6 us
  Pallas kernels  79 us (99%)
    pallas_call x1, Pallas kernels, per_device(): pl.pallas_call(functools.partial(kernel, nz, nd, ny), out_shape=(jax.Shap...  76.8 us
    pallas_call x1, Pallas kernels, per_device(): pl.pallas_call(write_out, out_shape=tuple((jax.ShapeDtypeStruct(v.shape,...  2.21 us

profile of v2, /device:TPU:1, one launch (start us, length us, event | category | flops | bytes accessed | tf_op | source)
XLA Modules:
  0.0 79.6 jit_solution(7835724307326805310)
XLA Ops:
  0.6 76.8 %shard_map.110 = (bf16[12,448]{1,0:T(8,128)(2,1)}, bf16[12,448]{1,0:T(8,128)(2,1)}, bf16[64,3584]{1,0:T(8,128)(2,1)}, bf16[64,3584]{1,0:T(8,128)(2,1)}, bf16[448,512]{1,0:T(8,128)(2,1)}) custom-call(bf16[12,448]{1,0:T(8,128)(2,1)} %tok_ref.1, s32[8,12]{1,0:T(8,128)} %bitcast.15, f32[8,12]{1,0:T(8,128)} %bitcast.16, bf16[64,3584]{1,0:T(8,128)(2,1)} %bitcast.12, ...), custom_call_target="tpu_custom_call" | custom-call | tf_op jit(solution)/shard_map/pallas_call | solution.py:484
  77.4 2.2 %shard_map.111 = (bf16[12,448]{1,0:T(8,128)(2,1)}, bf16[12,448]{1,0:T(8,128)(2,1)}, bf16[64,3584]{1,0:T(8,128)(2,1)}, bf16[64,3584]{1,0:T(8,128)(2,1)}, bf16[448,512]{1,0:T(8,128)(2,1)}) custom-call(bf16[12,448]{1,0:T(8,128)(2,1)} %get-tuple-element.15.refs_0_, bf16[12,448]{1,0:T(8,128)(2,1)} %get-tuple-element.16.refs_1_, ...), custom_call_target="tpu_custom_call" | custom-call | tf_op jit(solution)/shard_map/pallas_call | solution.py:551

commit v3 on v2

--- a/solution.py
+++ b/solution.py
@@ -70,6 +70,7 @@
     a_send,
     a_recv,
     b_send,
+    x_buf,
     dy_buf,
     x_all,
     w_raw,
@@ -219,7 +220,6 @@
     a_x = stage_a(0)
     rows_dy = (mm(gate_hi, og16[...]) + mm(gate_lo, og16[...])).astype(BF16)
     a_send[1] = rows_dy.reshape(nz, 2 * nd, feat)
-    a_dy = stage_a(1)
     peer_d = remote(wd_ref, wd_raw.at[1], other)
     peer_g = remote(wg_ref, w_raw.at[1], other)
     peer_u = remote(wu_ref, w_raw.at[3], other)
@@ -232,11 +232,11 @@
     cut(0)
     own[2].wait()
     cut(2)
-    b_x = stage_b(0, a_x, x_all.at[y])
-    b_dy = stage_b(1, a_dy, dy_buf)
-
-    nh = nd // 2
-    chunks = (slice(0, nh), slice(nh, nd))
+    b_x = stage_b(0, a_x, x_buf)
+    a_dy = stage_a(1)
+
+    nh = half_rows // 2
+    chunks = (slice(0, nh), slice(nh, half_rows))
     ways = ((0, 1), (1, -1))
     arriving = {}
 
@@ -245,8 +245,14 @@
         block = x_all.at[b, chunks[ch]]
         arriving[s, ch, way] = remote(block, block, at_y(sign)[1])
 
+    def pack(v):
+        return jnp.concatenate([v[0:half_rows], v[half_rows:rows]], axis=1)
+
+    def unpack(v):
+        return jnp.concatenate([v[:, 0:feat], v[:, feat : 2 * feat]], axis=0)
+
     def rows_of(b):
-        return x_all[b].reshape(rows, feat)
+        return unpack(x_all[b])
 
     def ring_step(s):
         for ch in range(2):
@@ -258,10 +264,11 @@
             b = lax.rem(y - sign * s + ny, ny)
             acc[...] += mm(rows_of(b), w_blk[b], NT)
 
-    top_half, low_half = slice(0, half_rows), slice(half_rows, rows)
-    halves = (top_half, low_half)
+    def halves_of(n):
+        return slice(0, n // 2), slice(n // 2, n)
 
     def tree_far(part, send, recv):
+        halves = halves_of(send.shape[2])
         far = {}
         p = part(4).astype(BF16)
         for way, sign in ways:
@@ -282,6 +289,7 @@
         return near
 
     def tree_mid(part, send, recv, far):
+        halves = halves_of(send.shape[2])
         mid = []
         for way, sign in ways:
             p = part(2 * sign)
@@ -309,9 +317,11 @@
 
     for copy in b_x:
         copy.wait_recv()
+    x_all[y] = pack(x_buf[...].reshape(rows, feat))
     for ch in range(2):
         for way, sign in ways:
             ring_send(0, ch, way, sign)
+    b_dy = stage_b(1, a_dy, dy_buf)
 
     own[0].wait()
     peer_d.wait_recv()
@@ -350,25 +360,27 @@
     act = a * sigma
     slope = sigma * (1.0 + a * (1.0 - sigma))
     h_cat[:, lanes(y)] = (act * b).astype(BF16)
+
+    def h_send(dist, hops, half=None):
+        out = []
+        for way, sign in ways:
+            b = lax.rem(y - sign * dist + ny, ny)
+            part = slice(0, rows) if half is None else halves_of(rows)[way]
+            block = h_cat.at[part, lanes(b)]
+            out.append(remote(block, block, at_y(sign * hops)[1]))
+        return out
+
+    h_two = h_send(0, 2)
+    h_one = h_send(0, 1)
     dh = tree_end(dh_part, dh_recv, dh_near, dh_mid)
     dab = jnp.concatenate(
         [(dh * b * slope).astype(BF16), (dh * act).astype(BF16)], axis=1
     )
 
     def dx_part(k):
-        return mm(dab, w_blk[at_y(k)[0]])
-
-    def h_send(dist, hops, half=None):
-        out = []
-        for way, sign in ways:
-            b = lax.rem(y - sign * dist + ny, ny)
-            block = h_cat.at[:, lanes(b)] if half is None else h_cat.at[halves[way], lanes(b)]
-            out.append(remote(block, block, at_y(sign * hops)[1]))
-        return out
+        return pack(mm(dab, w_blk[at_y(k)[0]]))
 
     dx_far = tree_far(dx_part, rs_send, rs_recv)
-    h_two = h_send(0, 2)
-    h_one = h_send(0, 1)
     dx_near = tree_near(dx_part, rs_send, rs_recv)
 
     def back_b(n, value):
@@ -413,7 +425,7 @@
         keep_d[:, span] = g[:, b * width : b * width + hid]
         give_d[:, span] = g[:, b * width + hid : (b + 1) * width].astype(BF16)
     give_d_copy = remote(give_d, got_d, other)
-    dx_b = back_b(1, tree_end(dx_part, rs_recv, dx_near, dx_mid))
+    dx_b = back_b(1, unpack(tree_end(dx_part, rs_recv, dx_near, dx_mid)))
     out_a = back_a(0, out_b)
 
     give_copy.wait_recv()
@@ -511,7 +523,8 @@
             pltpu.VMEM((2, nz, 2 * nd, feat), BF16),
             pltpu.VMEM((2, nd, 2 * nz, feat), BF16),
             pltpu.VMEM((nd, 2 * nz, feat), BF16),
-            pltpu.VMEM((ny, nd, 2 * nz, feat), BF16),
+            pltpu.VMEM((nd, 2 * nz, feat), BF16),
+            pltpu.VMEM((ny, rows // 2, 2 * feat), BF16),
             pltpu.VMEM((4, hid, width), BF16),
             pltpu.VMEM((ny, 4 * hid, feat), BF16),
             pltpu.VMEM((feat, 2 * ny * hid), BF16),
@@ -519,8 +532,8 @@
             pltpu.VMEM((2, 4, rows, 2 * hid), BF16),
             pltpu.VMEM((2, 4, rows, 2 * hid), BF16),
             pltpu.VMEM((rows, ny * 2 * hid), BF16),
-            pltpu.VMEM((2, 4, rows, feat), BF16),
-            pltpu.VMEM((2, 4, rows, feat), BF16),
+            pltpu.VMEM((2, 4, rows // 2, 2 * feat), BF16),
+            pltpu.VMEM((2, 4, rows // 2, 2 * feat), BF16),
             pltpu.VMEM((2, nd, 2 * nz, feat), BF16),
             pltpu.VMEM((2, nd, 2 * nz, feat), BF16),
             pltpu.VMEM((2, nz, 2 * nd, feat), BF16),

time: 79.9 us -> 76.8 us (0.961)
  Pallas kernels: 79 us -> 75.9 us
    pallas_call x1, Pallas kernels: 76.8 us -> 73.7 us  [per_device(): pl.pallas_call(functools.partial(kernel, nz, nd, ny), out_shape=(jax.Shap...]
where the time goes in v3:
time: 76.8 us; the launch traced here: 76.5 us
  Pallas kernels  75.9 us (99%)
    pallas_call x1, Pallas kernels, per_device(): pl.pallas_call(functools.partial(kernel, nz, nd, ny), out_shape=(jax.Shap...  73.7 us
    pallas_call x1, Pallas kernels, per_device(): pl.pallas_call(write_out, out_shape=tuple((jax.ShapeDtypeStruct(v.shape,...  2.21 us

profile of v3, /device:TPU:1, one launch (start us, length us, event | category | flops | bytes accessed | tf_op | source)
XLA Modules:
  0.0 76.5 jit_solution(15141587116957111842)
XLA Ops:
  0.6 73.7 %shard_map.110 = (bf16[12,448]{1,0:T(8,128)(2,1)}, bf16[12,448]{1,0:T(8,128)(2,1)}, bf16[64,3584]{1,0:T(8,128)(2,1)}, bf16[64,3584]{1,0:T(8,128)(2,1)}, bf16[448,512]{1,0:T(8,128)(2,1)}) custom-call(bf16[12,448]{1,0:T(8,128)(2,1)} %tok_ref.1, s32[8,12]{1,0:T(8,128)} %bitcast.15, f32[8,12]{1,0:T(8,128)} %bitcast.16, bf16[64,3584]{1,0:T(8,128)(2,1)} %bitcast.12, ...), custom_call_target="tpu_custom_call" | custom-call | tf_op jit(solution)/shard_map/pallas_call | solution.py:496
  74.3 2.2 %shard_map.111 = (bf16[12,448]{1,0:T(8,128)(2,1)}, bf16[12,448]{1,0:T(8,128)(2,1)}, bf16[64,3584]{1,0:T(8,128)(2,1)}, bf16[64,3584]{1,0:T(8,128)(2,1)}, bf16[448,512]{1,0:T(8,128)(2,1)}) custom-call(bf16[12,448]{1,0:T(8,128)(2,1)} %get-tuple-element.15.refs_0_, bf16[12,448]{1,0:T(8,128)(2,1)} %get-tuple-element.16.refs_1_, ...), custom_call_target="tpu_custom_call" | custom-call | tf_op jit(solution)/shard_map/pallas_call | solution.py:564

commit v4 on v3

--- a/solution.py
+++ b/solution.py
@@ -345,9 +345,9 @@
         return mm(dy, wd_all[:, lanes(at_y(k)[0])])
 
     dh_far = tree_far(dh_part, dh_send, dh_recv)
-    dh_near = tree_near(dh_part, dh_send, dh_recv)
     ring_step(2)
     dh_mid = tree_mid(dh_part, dh_send, dh_recv, dh_far)
+    dh_near = tree_near(dh_part, dh_send, dh_recv)
     ring_step(3)
     for way in range(2):
         arriving[hs - 1, way, way].wait_recv()
@@ -371,7 +371,6 @@
         return out
 
     h_two = h_send(0, 2)
-    h_one = h_send(0, 1)
     dh = tree_end(dh_part, dh_recv, dh_near, dh_mid)
     dab = jnp.concatenate(
         [(dh * b * slope).astype(BF16), (dh * act).astype(BF16)], axis=1
@@ -381,7 +380,7 @@
         return pack(mm(dab, w_blk[at_y(k)[0]]))
 
     dx_far = tree_far(dx_part, rs_send, rs_recv)
-    dx_near = tree_near(dx_part, rs_send, rs_recv)
+    h_one = h_send(0, 1)
 
     def back_b(n, value):
         ret_send[n] = value.astype(BF16).reshape(nd, 2 * nz, feat)
@@ -416,17 +415,18 @@
     h_three = h_send(2, 1)
     h_four = h_send(2, 2, half=True)
     dx_mid = tree_mid(dx_part, rs_send, rs_recv, dx_far)
+    dx_near = tree_near(dx_part, rs_send, rs_recv)
     for copy in h_one + h_three + h_four:
         copy.wait_recv()
     out_b = back_b(0, mm(h_cat[...], wd_all[...], NT))
+    dx_b = back_b(1, unpack(tree_end(dx_part, rs_recv, dx_near, dx_mid)))
+    out_a = back_a(0, out_b)
     g = mm(dy, h_cat[...], TN)
     for b in range(ny):
         span = slice(b * hid, (b + 1) * hid)
         keep_d[:, span] = g[:, b * width : b * width + hid]
         give_d[:, span] = g[:, b * width + hid : (b + 1) * width].astype(BF16)
     give_d_copy = remote(give_d, got_d, other)
-    dx_b = back_b(1, unpack(tree_end(dx_part, rs_recv, dx_near, dx_mid)))
-    out_a = back_a(0, out_b)
 
     give_copy.wait_recv()
     for b in range(ny):

time: 76.8 us -> 74.3 us (0.967)
  Pallas kernels: 75.9 us -> 73.4 us
    pallas_call x1, Pallas kernels: 73.7 us -> 71.2 us  [per_device(): pl.pallas_call(functools.partial(kernel, nz, nd, ny), out_shape=(jax.Shap...]
where the time goes in v4:
time: 74.3 us; the launch traced here: 74 us
  Pallas kernels  73.4 us (99%)
    pallas_call x1, Pallas kernels, per_device(): pl.pallas_call(functools.partial(kernel, nz, nd, ny), out_shape=(jax.Shap...  71.2 us
    pallas_call x1, Pallas kernels, per_device(): pl.pallas_call(write_out, out_shape=tuple((jax.ShapeDtypeStruct(v.shape,...  2.21 us

profile of v4, /device:TPU:1, one launch (start us, length us, event | category | flops | bytes accessed | tf_op | source)
XLA Modules:
  0.0 74.0 jit_solution(3044810227074127130)
XLA Ops:
  0.6 71.2 %shard_map.110 = (bf16[12,448]{1,0:T(8,128)(2,1)}, bf16[12,448]{1,0:T(8,128)(2,1)}, bf16[64,3584]{1,0:T(8,128)(2,1)}, bf16[64,3584]{1,0:T(8,128)(2,1)}, bf16[448,512]{1,0:T(8,128)(2,1)}) custom-call(bf16[12,448]{1,0:T(8,128)(2,1)} %tok_ref.1, s32[8,12]{1,0:T(8,128)} %bitcast.15, f32[8,12]{1,0:T(8,128)} %bitcast.16, bf16[64,3584]{1,0:T(8,128)(2,1)} %bitcast.12, ...), custom_call_target="tpu_custom_call" | custom-call | tf_op jit(solution)/shard_map/pallas_call | solution.py:496
  71.8 2.2 %shard_map.111 = (bf16[12,448]{1,0:T(8,128)(2,1)}, bf16[12,448]{1,0:T(8,128)(2,1)}, bf16[64,3584]{1,0:T(8,128)(2,1)}, bf16[64,3584]{1,0:T(8,128)(2,1)}, bf16[448,512]{1,0:T(8,128)(2,1)}) custom-call(bf16[12,448]{1,0:T(8,128)(2,1)} %get-tuple-element.15.refs_0_, bf16[12,448]{1,0:T(8,128)(2,1)} %get-tuple-element.16.refs_1_, ...), custom_call_target="tpu_custom_call" | custom-call | tf_op jit(solution)/shard_map/pallas_call | solution.py:564
